TPU v7x, 128 devices: a whole 4x4x4 slice. The times are simulated.
128 devices in a mesh: dp: 4 (over x), expert: 32 (over z, y, core).
Axes of the slice: x: 4, y: 4, z: 4, core: 2. Of those that a mesh axis runs over, the one named last changes fastest.
Arguments:
- tokens: bfloat16 [4096, 7168], P('expert', 'dp'), may hold values from -6 to 6
- cotangent: bfloat16 [4096, 7168], P('expert', 'dp'), may hold values from -6 to 6
- routes: int32 [4096, 4], P('expert'), may hold values from 0 to 31, all different within a row; in each aligned block of 128 rows (0 to 127, 128 to 255, ...) at most 24 rows name the same one
- gates: float32 [4096, 4], P('expert'), may hold values from 0.2 to 1
- w_gate: bfloat16 [32, 7168, 1024], P('expert', 'dp'), may hold values from -0.0625 to 0.0625
- w_up: bfloat16 [32, 7168, 1024], P('expert', 'dp'), may hold values from -0.0625 to 0.0625
- w_down: bfloat16 [32, 1024, 7168], P('expert', None, 'dp'), may hold values from -0.1875 to 0.1875
Outputs:
- mixed: bfloat16 [4096, 7168], P('expert', 'dp')
- input_grad: bfloat16 [4096, 7168], P('expert', 'dp')
- grad_w_gate: bfloat16 [32, 7168, 1024], P('expert', 'dp')
- grad_w_up: bfloat16 [32, 7168, 1024], P('expert', 'dp')
- grad_w_down: bfloat16 [32, 1024, 7168], P('expert', None, 'dp')
Inputs may be any that keep to these rules, and one draw needn't show every extreme that they name: `routes`: A row names 4 different experts; in each aligned block of 128 rows (the tokens of one index of expert) no expert is named by more than 24 rows, a bound that some block reaches.
All inputs are finite; a program needn't handle non-finite values.
Results may differ from a plain program's by a relative error of at most 0.019.
Values may be sent and summed in bfloat16 or wider, within the bound.
A program may use at most 128 MiB of HBM per device.

v0:
```python
import functools

import jax
import jax.numpy as jnp
from jax import lax
from jax.experimental import pallas as pl
from jax.experimental.pallas import tpu as pltpu
from jax.sharding import PartitionSpec as P

MESH = pl.DeviceIdType.MESH
BF = jnp.bfloat16
F32 = jnp.float32

TB = 128
TOP = 4
E = 32
CAP = 24
PAIR = 2 * CAP
D = 1792
HD = D // 2
H = 1024
ROWS = 768
NCH = 4
CH = ROWS // NCH
W3 = 3 * H
HW = W3 // 2
NN = (((1,), (0,)), ((), ()))
NT = (((1,), (1,)), ((), ()))
TN = (((0,), (0,)), ((), ()))


def mm(a, b, dims):
    return lax.dot_general(a, b, dims, preferred_element_type=F32)


def kernel(
    a1, a2, tok, cot, wg, wu, wd,
    mixed, ingrad, ogg, ogu, ogd,
    p1, p2, tokp, xd_send, xd_rows, part, r1, r2, act, or_send, or_recv, pt, res, vg, vu, vd,
    pair_s, pair_r, loc, wsem, ds_s, ds_r, x_s, x_r, cb_s, cb_r, fin_s, fin_r, fin_l, gsem,
):
    q = lax.axis_index("dp")
    e = lax.axis_index("expert")
    chip = e // 2
    core = e % 2
    other = 1 - core
    cz, cy = chip // 4, chip % 4
    right, left, opp = (q + 1) % 4, (q + 3) % 4, (q + 2) % 4
    partner = chip * 2 + other

    def to_chip(j):
        a, b = j // 4, j % 4
        return ((cz + a + b) % 4) * 4 + (cy + b) % 4

    def from_chip(j):
        a, b = j // 4, j % 4
        return ((cz + 8 - a - b) % 4) * 4 + (cy + 4 - b) % 4

    def half(c):
        return pl.ds(pl.multiple_of(c * HD, 128), HD)

    def rows48(j):
        return pl.ds(pl.multiple_of(j * PAIR, 16), PAIR)

    def blk(c):
        return pl.ds(pl.multiple_of(c * TB, TB), TB)

    local = [
        pltpu.make_async_copy(a1, p1.at[core], loc.at[0]),
        pltpu.make_async_copy(a2, p2.at[core], loc.at[1]),
        pltpu.make_async_copy(tok.at[:, half(core)], tokp.at[0, blk(core), :], loc.at[2]),
        pltpu.make_async_copy(cot.at[:, half(core)], tokp.at[1, blk(core), :], loc.at[3]),
    ]
    for cp in local:
        cp.start()

    bar = pltpu.get_barrier_semaphore()

    def greet(j, carry):
        d = to_chip(j)
        for k in range(2):
            pl.semaphore_signal(
                bar, inc=1, device_id={"dp": q, "expert": d * 2 + k}, device_id_type=MESH
            )
        return carry

    pl.semaphore_signal(bar, inc=1, device_id={"dp": q, "expert": partner}, device_id_type=MESH)
    for n in (right, left, opp):
        pl.semaphore_signal(bar, inc=1, device_id={"dp": n, "expert": e}, device_id_type=MESH)
    lax.fori_loop(1, 16, greet, 0)
    pl.semaphore_wait(bar, 34)

    def remote(src, dst, ss, rs, dp, ex):
        return pltpu.make_async_remote_copy(
            src_ref=src, dst_ref=dst, send_sem=ss, recv_sem=rs,
            device_id={"dp": dp, "expert": ex}, device_id_type=MESH,
        )

    def pair_copies(c):
        return [
            remote(a1, p1.at[c], pair_s.at[0], pair_r.at[0], q, partner),
            remote(a2, p2.at[c], pair_s.at[1], pair_r.at[1], q, partner),
            remote(tok.at[:, half(1 - c)], tokp.at[0, blk(c), :], pair_s.at[2], pair_r.at[2], q, partner),
            remote(cot.at[:, half(1 - c)], tokp.at[1, blk(c), :], pair_s.at[3], pair_r.at[3], q, partner),
        ]

    mine = pair_copies(core)
    for cp in mine:
        cp.start()
    weights = [
        pltpu.make_async_copy(wg, vg, wsem.at[0]),
        pltpu.make_async_copy(wu, vu, wsem.at[1]),
        pltpu.make_async_copy(wd, vd, wsem.at[2]),
    ]
    for cp in weights:
        cp.start()
    for cp in local:
        cp.wait()
    for cp in pair_copies(other):
        cp.wait_recv()

    def hits(row):
        return jnp.concatenate([p1[0, row : row + 1, :], p1[1, row : row + 1, :]], axis=1)

    def fill(j):
        d = to_chip(j)
        rid = (lax.broadcasted_iota(jnp.int32, (2 * PAIR, 2 * TB), 0) + d * (2 * PAIR)).astype(F32)
        one = jnp.zeros((2 * PAIR, 2 * TB), F32)
        gat = jnp.zeros((2 * PAIR, 2 * TB), F32)
        for k in range(TOP):
            hit = rid == hits(k)
            one = jnp.where(hit, 1.0, one)
            gat = jnp.where(hit, hits(8 + k), gat)
        xs = mm(one.astype(BF), tokp[0], NN).astype(BF)
        dsv = mm(gat.astype(BF), tokp[1], NN).astype(BF)
        xd_send[j, :, 0] = xs.reshape(2, PAIR, HD)
        xd_send[j, :, 1] = dsv.reshape(2, PAIR, HD)

    def disp(j, k, dst_chip, c_src):
        c_dst = core if k == 0 else other
        return remote(
            xd_send.at[j, c_dst], xd_rows.at[:, rows48(j), half(c_src)],
            ds_s.at[j, k], ds_r.at[j, k], q, dst_chip * 2 + c_dst,
        )

    fill(0)
    own = pltpu.make_async_copy(xd_send.at[0, core], xd_rows.at[:, rows48(0), half(core)], loc.at[4])
    own.start()
    disp(0, 1, chip, core).start()

    def send_one(j, carry):
        fill(j)
        d = to_chip(j)
        disp(j, 0, d, core).start()
        disp(j, 1, d, core).start()
        return carry

    lax.fori_loop(1, 16, send_one, 0)

    def build(n, carry):
        cols = pl.ds(pl.multiple_of(n * 256, 256), 256)
        cid = (lax.broadcasted_iota(jnp.int32, (TB, 256), 1) + n * 256).astype(F32)
        for b in range(2):
            one = jnp.zeros((TB, 256), F32)
            gat = jnp.zeros((TB, 256), F32)
            for k in range(TOP):
                hit = cid == p2[b, :, k : k + 1]
                one = jnp.where(hit, 1.0, one)
                gat = jnp.where(hit, p2[b, :, TOP + k : TOP + k + 1], gat)
            pt[0, b * TB : (b + 1) * TB, cols] = gat.astype(BF)
            pt[1, b * TB : (b + 1) * TB, cols] = one.astype(BF)
        return carry

    lax.fori_loop(0, E * PAIR // 256, build, 0)

    for cp in weights:
        cp.wait()

    def cols256(n):
        return pl.ds(pl.multiple_of(n * 256, 256), 256)

    def chunk(a):
        return pl.ds(a * CH, CH)

    def step_a(a):
        for j in range(4 * a, 4 * a + 4):
            if j == 0:
                own.wait()
            else:
                disp(j, 0, chip, core).wait_recv()
            disp(j, 1, chip, other).wait_recv()

        def body(n, carry):
            cs = cols256(n)
            x = xd_rows[0, chunk(a), :]
            part[a, :, :, cs] = mm(x, vg[:, cs], NN).astype(BF).reshape(4, PAIR, 256)
            part[a, :, :, pl.ds(pl.multiple_of(n * 256 + H, 256), 256)] = (
                mm(x, vu[:, cs], NN).astype(BF).reshape(4, PAIR, 256)
            )
            part[a, :, :, pl.ds(pl.multiple_of(n * 256 + 2 * H, 256), 256)] = (
                mm(xd_rows[1, chunk(a), :], vd[cs, :], NT).astype(BF).reshape(4, PAIR, 256)
            )
            return carry

        lax.fori_loop(0, H // 256, body, 0)
        for cp in rs1(a):
            cp.start()

    def rs1(a):
        return [
            remote(part.at[a, opp, :, pl.ds(0, HW)], r1.at[a, 0], x_s.at[a, 0], x_r.at[a, 0], right, e),
            remote(part.at[a, opp, :, pl.ds(HW, HW)], r1.at[a, 1], x_s.at[a, 1], x_r.at[a, 1], left, e),
        ]

    def rs2(a):
        return [
            remote(part.at[a, right], r2.at[a, 0], x_s.at[a, 2], x_r.at[a, 2], right, e),
            remote(part.at[a, left], r2.at[a, 1], x_s.at[a, 3], x_r.at[a, 3], left, e),
        ]

    def arow(a, n):
        return pl.ds(pl.multiple_of(a * CH + n * PAIR, 16), PAIR)

    def ag1(a, n):
        blkr = act.at[arow(a, n), :]
        return [
            remote(blkr, blkr, x_s.at[a, 4], x_r.at[a, 4], right, e),
            remote(blkr, blkr, x_s.at[a, 5], x_r.at[a, 5], left, e),
        ]

    def ag2(a, n0, n1):
        b0 = act.at[arow(a, n0), pl.ds(0, HW)]
        b1 = act.at[arow(a, n1), pl.ds(HW, HW)]
        return [
            remote(b0, b0, x_s.at[a, 6], x_r.at[a, 6], right, e),
            remote(b1, b1, x_s.at[a, 7], x_r.at[a, 7], left, e),
        ]

    def step_b(a):
        for cp in rs1(a):
            cp.wait_recv()
        s2 = rs2(a)
        part[a, right, :, 0:HW] = (part[a, right, :, 0:HW].astype(F32) + r1[a, 0].astype(F32)).astype(BF)
        s2[0].start()
        part[a, left, :, HW:W3] = (part[a, left, :, HW:W3].astype(F32) + r1[a, 1].astype(F32)).astype(BF)
        s2[1].start()

    def step_c(a):
        for cp in rs2(a):
            cp.wait_recv()

        def total(lo):
            s = slice(lo, lo + H)
            return part[a, q, :, s].astype(F32) + r2[a, 0, :, s].astype(F32) + r2[a, 1, :, s].astype(F32)

        g, u, hg = total(0), total(H), total(2 * H)
        sig = jax.nn.sigmoid(g)
        act[arow(a, q), 0:H] = (g * sig * u).astype(BF)
        act[arow(a, q), H : 2 * H] = (hg * u * sig * (1.0 + g * (1.0 - sig))).astype(BF)
        act[arow(a, q), 2 * H : W3] = (hg * g * sig).astype(BF)
        for cp in ag1(a, q):
            cp.start()

    def step_d(a):
        ag1(a, left)[0].wait_recv()
        ag1(a, right)[1].wait_recv()
        for cp in ag2(a, left, right):
            cp.start()

    def comb(j, k, dst_chip, src_e):
        c_dst = core if k == 0 else other
        return remote(
            or_send.at[:, rows48(j), half(c_dst)], or_recv.at[:, rows48(src_e), :],
            cb_s.at[j, k], cb_r.at[j, k], q, dst_chip * 2 + c_dst,
        )

    own_back = pltpu.make_async_copy(or_send.at[:, rows48(0), half(core)], or_recv.at[:, rows48(e), :], loc.at[5])

    def step_e(a):
        for cp in ag2(a, opp, opp):
            cp.wait_recv()

        def body(n, carry):
            cs = cols256(n)
            or_send[0, chunk(a), cs] = mm(act[chunk(a), 0:H], vd[:, cs], NN).astype(BF)
            or_send[1, chunk(a), cs] = (
                mm(act[chunk(a), H : 2 * H], vg[cs, :], NT) + mm(act[chunk(a), 2 * H : W3], vu[cs, :], NT)
            ).astype(BF)
            return carry

        lax.fori_loop(0, D // 256, body, 0)
        for j in range(4 * a, 4 * a + 4):
            d = from_chip(j)
            if j == 0:
                own_back.start()
            else:
                comb(j, 0, d, e).start()
            comb(j, 1, d, e).start()

    for step, a in (
        (step_a, 0), (step_b, 0), (step_c, 0), (step_a, 1), (step_d, 0), (step_b, 1), (step_e, 0), (step_c, 1),
        (step_a, 2), (step_d, 1), (step_b, 2), (step_e, 1), (step_c, 2), (step_a, 3), (step_d, 2), (step_b, 3),
        (step_e, 2), (step_c, 3), (step_d, 3), (step_e, 3),
    ):
        step(a)

    def grad_x(n, carry):
        cs = cols256(n)
        x = xd_rows[0, :, cs]
        vg[cs, :] = mm(x, act[:, H : 2 * H], TN).astype(BF)
        vu[cs, :] = mm(x, act[:, 2 * H : W3], TN).astype(BF)
        return carry

    lax.fori_loop(0, D // 256, grad_x, 0)
    out_w = [
        pltpu.make_async_copy(vg, ogg, gsem.at[0]),
        pltpu.make_async_copy(vu, ogu, gsem.at[1]),
        pltpu.make_async_copy(vd, ogd, gsem.at[2]),
    ]
    out_w[0].start()
    out_w[1].start()

    def grad_d(n, carry):
        cs = cols256(n)
        vd[cs, :] = mm(act[:, cs], xd_rows[1], TN).astype(BF)
        return carry

    lax.fori_loop(0, H // 256, grad_d, 0)
    out_w[2].start()

    def arrived(j, carry):
        src = to_chip(j)
        comb(j, 0, chip, src * 2 + core).wait_recv()
        comb(j, 1, chip, src * 2 + other).wait_recv()
        return carry

    own_back.wait()
    comb(0, 1, chip, chip * 2 + other).wait_recv()
    lax.fori_loop(1, 16, arrived, 0)
    res[0] = mm(pt[0], or_recv[0], NN).astype(BF)
    res[1] = mm(pt[1], or_recv[1], NN).astype(BF)
    fin = []
    for k, out in enumerate((mixed, ingrad)):
        away = remote(res.at[k, blk(other), :], out.at[:, half(core)], fin_s.at[k], fin_r.at[k], q, partner)
        here = pltpu.make_async_copy(res.at[k, blk(core), :], out.at[:, half(core)], fin_l.at[k])
        away.start()
        here.start()
        fin.append((away, here))

    for cp in mine:
        cp.wait_send()
    disp(0, 1, chip, core).wait_send()
    comb(0, 1, chip, e).wait_send()

    def sent(j, carry):
        for k in range(2):
            disp(j, k, chip, core).wait_send()
            comb(j, k, chip, e).wait_send()
        return carry

    lax.fori_loop(1, 16, sent, 0)
    for a in range(NCH):
        for cp in rs1(a) + rs2(a) + ag1(a, q) + ag2(a, left, right):
            cp.wait_send()
    for cp in out_w:
        cp.wait()
    for k, out in enumerate((mixed, ingrad)):
        fin[k][0].wait_send()
        fin[k][1].wait()
        remote(res.at[k, blk(core), :], out.at[:, half(other)], fin_s.at[k], fin_r.at[k], q, partner).wait_recv()


def local(tokens, cotangent, routes, gates, w_gate, w_up, w_down):
    core = lax.axis_index("expert") % 2
    ids = jnp.arange(E, dtype=jnp.int32)
    onehot = routes[:, :, None] == ids[None, None, :]
    named = jnp.any(onehot, axis=1).astype(BF)
    tri = (jnp.arange(TB)[:, None] > jnp.arange(TB)[None, :]).astype(BF)
    before = jnp.dot(tri, named, preferred_element_type=F32)
    slot = jnp.sum(jnp.where(onehot, before[:, None, :], 0.0), axis=2)
    target = routes.astype(F32) * PAIR + slot + (core * CAP).astype(F32)
    a2 = jnp.pad(jnp.concatenate([target, gates], axis=1), ((0, 0), (0, 128 - 2 * TOP)))
    pad = jnp.zeros((4, TB), F32)
    a1 = jnp.concatenate([target.T, pad, gates.T, pad], axis=0)

    any_spec = pl.BlockSpec(memory_space=pl.ANY)
    dma = pltpu.SemaphoreType.DMA
    out = pl.pallas_call(
        kernel,
        out_shape=(
            jax.ShapeDtypeStruct((TB, D), BF),
            jax.ShapeDtypeStruct((TB, D), BF),
            jax.ShapeDtypeStruct((D, H), BF),
            jax.ShapeDtypeStruct((D, H), BF),
            jax.ShapeDtypeStruct((H, D), BF),
        ),
        in_specs=[any_spec] * 7,
        out_specs=[any_spec] * 5,
        scratch_shapes=[
            pltpu.VMEM((2, 16, TB), F32),
            pltpu.VMEM((2, TB, 128), F32),
            pltpu.VMEM((2, 2 * TB, HD), BF),
            pltpu.VMEM((16, 2, 2, PAIR, HD), BF),
            pltpu.VMEM((2, ROWS, D), BF),
            pltpu.VMEM((NCH, 4, PAIR, W3), BF),
            pltpu.VMEM((NCH, 2, PAIR, HW), BF),
            pltpu.VMEM((NCH, 2, PAIR, W3), BF),
            pltpu.VMEM((ROWS, W3), BF),
            pltpu.VMEM((2, ROWS, D), BF),
            pltpu.VMEM((2, E * PAIR, HD), BF),
            pltpu.VMEM((2, 2 * TB, E * PAIR), BF),
            pltpu.VMEM((2, 2 * TB, HD), BF),
            pltpu.VMEM((D, H), BF),
            pltpu.VMEM((D, H), BF),
            pltpu.VMEM((H, D), BF),
            dma((4,)), dma((4,)), dma((6,)), dma((3,)),
            dma((16, 2)), dma((16, 2)), dma((NCH, 8)), dma((NCH, 8)),
            dma((16, 2)), dma((16, 2)), dma((2,)), dma((2,)), dma((2,)), dma((3,)),
        ],
        compiler_params=pltpu.CompilerParams(
            collective_id=0, has_side_effects=True, vmem_limit_bytes=62 * 1024 * 1024
        ),
    )(a1, a2, tokens, cotangent, w_gate.reshape(D, H), w_up.reshape(D, H), w_down.reshape(H, D))
    mixed, ingrad, gg, gu, gd = out
    return mixed, ingrad, gg[None], gu[None], gd[None]


def solution(mesh):
    in_specs = (
        P("expert", "dp"),
        P("expert", "dp"),
        P("expert", None),
        P("expert", None),
        P("expert", "dp", None),
        P("expert", "dp", None),
        P("expert", None, "dp"),
    )
    out_specs = (
        P("expert", "dp"),
        P("expert", "dp"),
        P("expert", "dp", None),
        P("expert", "dp", None),
        P("expert", None, "dp"),
    )
    return jax.shard_map(local, mesh=mesh, in_specs=in_specs, out_specs=out_specs, check_vma=False)
```

profile of v0, /device:TPU:43, one launch (start us, length us, event | category | flops | bytes accessed | tf_op | source)
XLA Modules:
  0.0 212.8 jit_solution(15190868158090236881)
XLA Ops:
  0.6 0.7 fusion
  1.3 0.1 fusion.1
  1.5 0.7 select_reduce_fusion
  2.2 0.7 add_add_fusion
  2.9 0.7 pad_maximum_fusion.1
  3.6 1.3 pad_maximum_fusion.a1
  4.9 0.1 copy.23
  5.0 0.6 pad.4.a2
  5.6 193.9 %shard_map.110 = (bf16[128,1792]{1,0:T(8,128)(2,1)}, bf16[128,1792]{1,0:T(8,128)(2,1)}, bf16[1792,1024]{1,0:T(8,128)(2,1)}, bf16[1792,1024]{1,0:T(8,128)(2,1)}, bf16[1024,1792]{1,0:T(8,128)(2,1)}) custom-call(f32[16,128]{1,0:T(8,128)} %pad_maximum_fusion.a1, f32[128,128]{1,0:T(8,128)} %pad.4.a2, bf16[128,1792]{1,0:T(8,128)(2,1)} %tok.1, ...), custom_call_target="tpu_custom_call" | custom-call | tf_op jit(solution)/shard_map/pallas_call | solution.py:388
  199.5 1.8 copy.29
  201.4 1.8 copy.30
  203.2 0.0 copy-start.1
  203.2 4.4 %copy.31 = bf16[1,1792,1024]{2,1,0:T(8,128)(2,1)} copy(bf16[1,1792,1024]{2,1,0:T(8,128)(2,1)} %bitcast.11) | data formatting | bytes 7340032
  207.6 0.0 copy-done.1
  207.6 0.0 copy-start
  207.6 1.9 copy.32
  209.5 1.5 copy-done
  211.0 1.8 copy.33
  (1 shorter events, 0.0 us)
Async XLA Ops:
  203.2 4.4 %copy-start.1 = (bf16[1792,1024]{1,0:T(8,128)(2,1)S(1)}, bf16[1792,1024]{1,0:T(8,128)(2,1)}, u32[]{:S(2)}) copy-start(bf16[1792,1024]{1,0:T(8,128)(2,1)} %get-tuple-element.13) | copy-start | bytes 11010052
  207.6 3.4 %copy-start = (bf16[1024,1792]{1,0:T(8,128)(2,1)S(1)}, bf16[1024,1792]{1,0:T(8,128)(2,1)}, u32[]{:S(2)}) copy-start(bf16[1024,1792]{1,0:T(8,128)(2,1)} %get-tuple-element.14) | copy-start | bytes 11010052
where the time goes:
time: 213 us
  Pallas kernels  194 us (91%)
  local copies, waits for them, and re-layouts  14 us (7%)
  other arithmetic  4.09 us (2%)
    pallas_call x1, Pallas kernels, local(): pl.pallas_call(kernel, out_shape=(jax.ShapeDtypeStruct((TB, D), BF), jax....  194 us
    unnamed x9, local copies, waits for them, and re-layouts  13.2 us

commit v1 on v0

--- a/solution.py
+++ b/solution.py
@@ -24,6 +24,12 @@
 CH = ROWS // NCH
 W3 = 3 * H
 HW = W3 // 2
+SLOTS = (
+    (0, 0), (1, 1), (1, 3), (3, 1),
+    (1, 2), (2, 1), (2, 3), (3, 2),
+    (3, 3), (2, 2), (0, 2), (2, 0),
+    (0, 1), (1, 0), (0, 3), (3, 0),
+)
 NN = (((1,), (0,)), ((), ()))
 NT = (((1,), (1,)), ((), ()))
 TN = (((0,), (0,)), ((), ()))
@@ -34,10 +40,10 @@
 
 
 def kernel(
-    a1, a2, tok, cot, wg, wu, wd,
+    routes, gates, tok, cot, wg, wu, wd,
     mixed, ingrad, ogg, ogu, ogd,
-    p1, p2, tokp, xd_send, xd_rows, part, r1, r2, act, or_send, or_recv, pt, res, vg, vu, vd,
-    pair_s, pair_r, loc, wsem, ds_s, ds_r, x_s, x_r, cb_s, cb_r, fin_s, fin_r, fin_l, gsem,
+    p1, tokp, xd_send, xd_rows, part, r1, r2, act, or_send, or_recv, pt, res, vg, vu, vd,
+    pair_s, pair_r, loc, wsem, ag_s, ag_r, ds_s, ds_r, x_s, x_r, cb_s, cb_r, fin_s, fin_r, fin_l, gsem,
 ):
     q = lax.axis_index("dp")
     e = lax.axis_index("expert")
@@ -48,13 +54,23 @@
     right, left, opp = (q + 1) % 4, (q + 3) % 4, (q + 2) % 4
     partner = chip * 2 + other
 
+    flip = core == 1
+    pa, pb = jnp.where(flip, cy, cz), jnp.where(flip, cz, cy)
+
+    def chip_at(a, b):
+        a, b = a % 4, b % 4
+        return jnp.where(flip, b * 4 + a, a * 4 + b)
+
+    def slot(a, b):
+        return jnp.where(flip, SLOTS.index((b, a)), SLOTS.index((a, b)))
+
     def to_chip(j):
-        a, b = j // 4, j % 4
-        return ((cz + a + b) % 4) * 4 + (cy + b) % 4
+        dz, dy = SLOTS[j]
+        return ((cz + dz) % 4) * 4 + (cy + dy) % 4
 
     def from_chip(j):
-        a, b = j // 4, j % 4
-        return ((cz + 8 - a - b) % 4) * 4 + (cy + 4 - b) % 4
+        dz, dy = SLOTS[j]
+        return ((cz + 4 - dz) % 4) * 4 + (cy + 4 - dy) % 4
 
     def half(c):
         return pl.ds(pl.multiple_of(c * HD, 128), HD)
@@ -66,28 +82,24 @@
         return pl.ds(pl.multiple_of(c * TB, TB), TB)
 
     local = [
-        pltpu.make_async_copy(a1, p1.at[core], loc.at[0]),
-        pltpu.make_async_copy(a2, p2.at[core], loc.at[1]),
-        pltpu.make_async_copy(tok.at[:, half(core)], tokp.at[0, blk(core), :], loc.at[2]),
-        pltpu.make_async_copy(cot.at[:, half(core)], tokp.at[1, blk(core), :], loc.at[3]),
+        pltpu.make_async_copy(tok.at[:, half(core)], tokp.at[0, 0, blk(core), :], loc.at[2]),
+        pltpu.make_async_copy(cot.at[:, half(core)], tokp.at[0, 1, blk(core), :], loc.at[3]),
     ]
     for cp in local:
         cp.start()
 
     bar = pltpu.get_barrier_semaphore()
 
-    def greet(j, carry):
-        d = to_chip(j)
-        for k in range(2):
-            pl.semaphore_signal(
-                bar, inc=1, device_id={"dp": q, "expert": d * 2 + k}, device_id_type=MESH
-            )
+    def greet(d, carry):
+        @pl.when(d != e)
+        def _():
+            pl.semaphore_signal(bar, inc=1, device_id={"dp": q, "expert": d}, device_id_type=MESH)
+
         return carry
 
-    pl.semaphore_signal(bar, inc=1, device_id={"dp": q, "expert": partner}, device_id_type=MESH)
     for n in (right, left, opp):
         pl.semaphore_signal(bar, inc=1, device_id={"dp": n, "expert": e}, device_id_type=MESH)
-    lax.fori_loop(1, 16, greet, 0)
+    lax.fori_loop(0, E, greet, 0)
     pl.semaphore_wait(bar, 34)
 
     def remote(src, dst, ss, rs, dp, ex):
@@ -98,15 +110,28 @@
 
     def pair_copies(c):
         return [
-            remote(a1, p1.at[c], pair_s.at[0], pair_r.at[0], q, partner),
-            remote(a2, p2.at[c], pair_s.at[1], pair_r.at[1], q, partner),
-            remote(tok.at[:, half(1 - c)], tokp.at[0, blk(c), :], pair_s.at[2], pair_r.at[2], q, partner),
-            remote(cot.at[:, half(1 - c)], tokp.at[1, blk(c), :], pair_s.at[3], pair_r.at[3], q, partner),
+            remote(tok.at[:, half(1 - c)], tokp.at[0, 0, blk(c), :], pair_s.at[2], pair_r.at[2], q, partner),
+            remote(cot.at[:, half(1 - c)], tokp.at[0, 1, blk(c), :], pair_s.at[3], pair_r.at[3], q, partner),
         ]
+
+    def pair_rows(c):
+        return remote(p1.at[0, c], p1.at[0, c], pair_s.at[0], pair_r.at[0], q, partner)
 
     mine = pair_copies(core)
     for cp in mine:
         cp.start()
+
+    ids = lax.broadcasted_iota(jnp.int32, (E, TB), 0)
+    picks = [routes[k : k + 1, :] == ids for k in range(TOP)]
+    named = functools.reduce(jnp.logical_or, picks)
+    earlier = lax.broadcasted_iota(jnp.int32, (TB, TB), 0) < lax.broadcasted_iota(jnp.int32, (TB, TB), 1)
+    before = mm(jnp.where(named, 1.0, 0.0).astype(BF), jnp.where(earlier, 1.0, 0.0).astype(BF), NN)
+    first = (core * CAP).astype(F32)
+    for k in range(TOP):
+        rank = jnp.sum(jnp.where(picks[k], before, 0.0), axis=0, keepdims=True)
+        p1[0, core, k : k + 1, :] = routes[k : k + 1, :].astype(F32) * PAIR + rank + first
+        p1[0, core, TOP + k : TOP + k + 1, :] = gates[k : k + 1, :]
+    pair_rows(core).start()
     weights = [
         pltpu.make_async_copy(wg, vg, wsem.at[0]),
         pltpu.make_async_copy(wu, vu, wsem.at[1]),
@@ -116,62 +141,83 @@
         cp.start()
     for cp in local:
         cp.wait()
-    for cp in pair_copies(other):
+    for cp in pair_copies(other) + [pair_rows(other)]:
         cp.wait_recv()
 
-    def hits(row):
-        return jnp.concatenate([p1[0, row : row + 1, :], p1[1, row : row + 1, :]], axis=1)
-
-    def fill(j):
-        d = to_chip(j)
+    def spread(a):
+        d = chip_at(pa + a, pb) * 2 + core
+        return [
+            remote(p1.at[0], p1.at[a], ag_s.at[a, 0], ag_r.at[a, 0], q, d),
+            remote(tokp.at[0], tokp.at[a], ag_s.at[a, 1], ag_r.at[a, 1], q, d),
+        ]
+
+    for a in (1, 3, 2):
+        for cp in spread(a):
+            cp.start()
+
+    def fill(a, b):
+        d = chip_at(pa, pb + b)
         rid = (lax.broadcasted_iota(jnp.int32, (2 * PAIR, 2 * TB), 0) + d * (2 * PAIR)).astype(F32)
         one = jnp.zeros((2 * PAIR, 2 * TB), F32)
         gat = jnp.zeros((2 * PAIR, 2 * TB), F32)
+
+        def of(row):
+            return jnp.concatenate([p1[a, 0, row : row + 1, :], p1[a, 1, row : row + 1, :]], axis=1)
+
         for k in range(TOP):
-            hit = rid == hits(k)
+            hit = rid == of(k)
             one = jnp.where(hit, 1.0, one)
-            gat = jnp.where(hit, hits(8 + k), gat)
-        xs = mm(one.astype(BF), tokp[0], NN).astype(BF)
-        dsv = mm(gat.astype(BF), tokp[1], NN).astype(BF)
-        xd_send[j, :, 0] = xs.reshape(2, PAIR, HD)
-        xd_send[j, :, 1] = dsv.reshape(2, PAIR, HD)
-
-    def disp(j, k, dst_chip, c_src):
+            gat = jnp.where(hit, of(TOP + k), gat)
+        xs = mm(one.astype(BF), tokp[a, 0], NN).astype(BF)
+        dsv = mm(gat.astype(BF), tokp[a, 1], NN).astype(BF)
+        xd_send[4 * a + b, :, 0] = xs.reshape(2, PAIR, HD)
+        xd_send[4 * a + b, :, 1] = dsv.reshape(2, PAIR, HD)
+
+    def disp(a, b, k):
         c_dst = core if k == 0 else other
+        j = slot(a, b)
+        src, dst = xd_send.at[4 * a + b, c_dst], xd_rows.at[:, rows48(j), half(core)]
+        if b == 0 and k == 0:
+            return pltpu.make_async_copy(src, dst, ds_r.at[j, 0])
+        return remote(src, dst, ds_s.at[j, k], ds_r.at[j, k], q, chip_at(pa, pb + b) * 2 + c_dst)
+
+    def from_other(a, b):
+        j = slot(a, b)
         return remote(
-            xd_send.at[j, c_dst], xd_rows.at[:, rows48(j), half(c_src)],
-            ds_s.at[j, k], ds_r.at[j, k], q, dst_chip * 2 + c_dst,
+            xd_send.at[4 * a + b, core], xd_rows.at[:, rows48(j), half(other)],
+            ds_s.at[j, 1], ds_r.at[j, 1], q, partner,
         )
 
-    fill(0)
-    own = pltpu.make_async_copy(xd_send.at[0, core], xd_rows.at[:, rows48(0), half(core)], loc.at[4])
-    own.start()
-    disp(0, 1, chip, core).start()
-
-    def send_one(j, carry):
-        fill(j)
-        d = to_chip(j)
-        disp(j, 0, d, core).start()
-        disp(j, 1, d, core).start()
+    have = {0}
+
+    def send_chunk(c):
+        for a, b in sorted(SLOTS[4 * c : 4 * c + 4], key=lambda ab: (0, 1, 3, 2)[ab[0]]):
+            if a not in have:
+                have.add(a)
+                for cp in spread(a):
+                    cp.wait_recv()
+            fill(a, b)
+            disp(a, b, 0).start()
+            disp(a, b, 1).start()
+
+    for c in range(NCH):
+        send_chunk(c)
+
+    def build(n, carry):
+        r = pl.ds(pl.multiple_of(n * 128, 128), 128)
+        rid = (lax.broadcasted_iota(jnp.int32, (128, TB), 0) + n * 128).astype(F32)
+        for b in range(2):
+            one = jnp.zeros((128, TB), F32)
+            gat = jnp.zeros((128, TB), F32)
+            for k in range(TOP):
+                hit = rid == p1[0, b, k : k + 1, :]
+                one = jnp.where(hit, 1.0, one)
+                gat = jnp.where(hit, p1[0, b, TOP + k : TOP + k + 1, :], gat)
+            pt[0, r, b * TB : (b + 1) * TB] = gat.astype(BF)
+            pt[1, r, b * TB : (b + 1) * TB] = one.astype(BF)
         return carry
 
-    lax.fori_loop(1, 16, send_one, 0)
-
-    def build(n, carry):
-        cols = pl.ds(pl.multiple_of(n * 256, 256), 256)
-        cid = (lax.broadcasted_iota(jnp.int32, (TB, 256), 1) + n * 256).astype(F32)
-        for b in range(2):
-            one = jnp.zeros((TB, 256), F32)
-            gat = jnp.zeros((TB, 256), F32)
-            for k in range(TOP):
-                hit = cid == p2[b, :, k : k + 1]
-                one = jnp.where(hit, 1.0, one)
-                gat = jnp.where(hit, p2[b, :, TOP + k : TOP + k + 1], gat)
-            pt[0, b * TB : (b + 1) * TB, cols] = gat.astype(BF)
-            pt[1, b * TB : (b + 1) * TB, cols] = one.astype(BF)
-        return carry
-
-    lax.fori_loop(0, E * PAIR // 256, build, 0)
+    lax.fori_loop(0, E * PAIR // 128, build, 0)
 
     for cp in weights:
         cp.wait()
@@ -183,12 +229,13 @@
         return pl.ds(a * CH, CH)
 
     def step_a(a):
-        for j in range(4 * a, 4 * a + 4):
-            if j == 0:
-                own.wait()
+        for sa, sb in SLOTS[4 * a : 4 * a + 4]:
+            mine_in = disp(sa, sb, 0)
+            if sb == 0:
+                mine_in.wait()
             else:
-                disp(j, 0, chip, core).wait_recv()
-            disp(j, 1, chip, other).wait_recv()
+                mine_in.wait_recv()
+            from_other(sa, sb).wait_recv()
 
         def body(n, carry):
             cs = cols256(n)
@@ -328,17 +375,14 @@
     lax.fori_loop(0, H // 256, grad_d, 0)
     out_w[2].start()
 
-    def arrived(j, carry):
+    own_back.wait()
+    for j in range(16):
         src = to_chip(j)
-        comb(j, 0, chip, src * 2 + core).wait_recv()
+        if j > 0:
+            comb(j, 0, chip, src * 2 + core).wait_recv()
         comb(j, 1, chip, src * 2 + other).wait_recv()
-        return carry
-
-    own_back.wait()
-    comb(0, 1, chip, chip * 2 + other).wait_recv()
-    lax.fori_loop(1, 16, arrived, 0)
-    res[0] = mm(pt[0], or_recv[0], NN).astype(BF)
-    res[1] = mm(pt[1], or_recv[1], NN).astype(BF)
+    res[0] = mm(pt[0], or_recv[0], TN).astype(BF)
+    res[1] = mm(pt[1], or_recv[1], TN).astype(BF)
     fin = []
     for k, out in enumerate((mixed, ingrad)):
         away = remote(res.at[k, blk(other), :], out.at[:, half(core)], fin_s.at[k], fin_r.at[k], q, partner)
@@ -347,18 +391,19 @@
         here.start()
         fin.append((away, here))
 
-    for cp in mine:
+    for cp in mine + [pair_rows(core)]:
         cp.wait_send()
-    disp(0, 1, chip, core).wait_send()
-    comb(0, 1, chip, e).wait_send()
-
-    def sent(j, carry):
-        for k in range(2):
-            disp(j, k, chip, core).wait_send()
-            comb(j, k, chip, e).wait_send()
-        return carry
-
-    lax.fori_loop(1, 16, sent, 0)
+    for a in (1, 2, 3):
+        for cp in spread(a):
+            cp.wait_send()
+    for a, b in SLOTS:
+        if b != 0:
+            disp(a, b, 0).wait_send()
+        disp(a, b, 1).wait_send()
+    for j in range(16):
+        if j > 0:
+            comb(j, 0, chip, e).wait_send()
+        comb(j, 1, chip, e).wait_send()
     for a in range(NCH):
         for cp in rs1(a) + rs2(a) + ag1(a, q) + ag2(a, left, right):
             cp.wait_send()
@@ -370,19 +415,25 @@
         remote(res.at[k, blk(core), :], out.at[:, half(other)], fin_s.at[k], fin_r.at[k], q, partner).wait_recv()
 
 
+def settle(i0, i1, i2, i3, i4, o0, o1, o2, o3, o4, b0, b1, b2, b3, b4, in_s, out_s):
+    loads, stores = [], []
+    for n, (i, b, o) in enumerate(zip((i2, i3, i4, i0, i1), (b2, b3, b4, b0, b1), (o2, o3, o4, o0, o1))):
+        step = i.shape[0] // 4
+        for k in range(4):
+            r = pl.ds(k * step, step)
+            loads.append(pltpu.make_async_copy(i.at[r, :], b.at[r, :], in_s.at[n, k]))
+            stores.append(pltpu.make_async_copy(b.at[r, :], o.at[r, :], out_s.at[n, k]))
+    for cp in loads:
+        cp.start()
+    for cp, st in zip(loads, stores):
+        cp.wait()
+        st.start()
+    for st in stores:
+        st.wait()
+
+
 def local(tokens, cotangent, routes, gates, w_gate, w_up, w_down):
-    core = lax.axis_index("expert") % 2
-    ids = jnp.arange(E, dtype=jnp.int32)
-    onehot = routes[:, :, None] == ids[None, None, :]
-    named = jnp.any(onehot, axis=1).astype(BF)
-    tri = (jnp.arange(TB)[:, None] > jnp.arange(TB)[None, :]).astype(BF)
-    before = jnp.dot(tri, named, preferred_element_type=F32)
-    slot = jnp.sum(jnp.where(onehot, before[:, None, :], 0.0), axis=2)
-    target = routes.astype(F32) * PAIR + slot + (core * CAP).astype(F32)
-    a2 = jnp.pad(jnp.concatenate([target, gates], axis=1), ((0, 0), (0, 128 - 2 * TOP)))
-    pad = jnp.zeros((4, TB), F32)
-    a1 = jnp.concatenate([target.T, pad, gates.T, pad], axis=0)
-
+    vmem = pl.BlockSpec(memory_space=pltpu.VMEM)
     any_spec = pl.BlockSpec(memory_space=pl.ANY)
     dma = pltpu.SemaphoreType.DMA
     out = pl.pallas_call(
@@ -394,12 +445,11 @@
             jax.ShapeDtypeStruct((D, H), BF),
             jax.ShapeDtypeStruct((H, D), BF),
         ),
-        in_specs=[any_spec] * 7,
+        in_specs=[vmem] * 2 + [any_spec] * 5,
         out_specs=[any_spec] * 5,
         scratch_shapes=[
-            pltpu.VMEM((2, 16, TB), F32),
-            pltpu.VMEM((2, TB, 128), F32),
-            pltpu.VMEM((2, 2 * TB, HD), BF),
+            pltpu.VMEM((4, 2, 2 * TOP, TB), F32),
+            pltpu.VMEM((4, 2, 2 * TB, HD), BF),
             pltpu.VMEM((16, 2, 2, PAIR, HD), BF),
             pltpu.VMEM((2, ROWS, D), BF),
             pltpu.VMEM((NCH, 4, PAIR, W3), BF),
@@ -408,20 +458,27 @@
             pltpu.VMEM((ROWS, W3), BF),
             pltpu.VMEM((2, ROWS, D), BF),
             pltpu.VMEM((2, E * PAIR, HD), BF),
-            pltpu.VMEM((2, 2 * TB, E * PAIR), BF),
+            pltpu.VMEM((2, E * PAIR, 2 * TB), BF),
             pltpu.VMEM((2, 2 * TB, HD), BF),
             pltpu.VMEM((D, H), BF),
             pltpu.VMEM((D, H), BF),
             pltpu.VMEM((H, D), BF),
-            dma((4,)), dma((4,)), dma((6,)), dma((3,)),
+            dma((4,)), dma((4,)), dma((6,)), dma((3,)), dma((4, 2)), dma((4, 2)),
             dma((16, 2)), dma((16, 2)), dma((NCH, 8)), dma((NCH, 8)),
             dma((16, 2)), dma((16, 2)), dma((2,)), dma((2,)), dma((2,)), dma((3,)),
         ],
         compiler_params=pltpu.CompilerParams(
             collective_id=0, has_side_effects=True, vmem_limit_bytes=62 * 1024 * 1024
         ),
-    )(a1, a2, tokens, cotangent, w_gate.reshape(D, H), w_up.reshape(D, H), w_down.reshape(H, D))
-    mixed, ingrad, gg, gu, gd = out
+    )(routes.T, gates.T, tokens, cotangent, w_gate.reshape(D, H), w_up.reshape(D, H), w_down.reshape(H, D))
+    mixed, ingrad, gg, gu, gd = pl.pallas_call(
+        settle,
+        out_shape=[jax.ShapeDtypeStruct(o.shape, o.dtype) for o in out],
+        in_specs=[pl.BlockSpec(memory_space=pltpu.HBM)] * 5,
+        out_specs=[any_spec] * 5,
+        scratch_shapes=[pltpu.VMEM((TB, D), BF), pltpu.VMEM((TB, D), BF), pltpu.VMEM((D, H), BF), pltpu.VMEM((D, H), BF), pltpu.VMEM((H, D), BF), dma((5, 4)), dma((5, 4))],
+        compiler_params=pltpu.CompilerParams(vmem_limit_bytes=60 * 1024 * 1024),
+    )(*out)
     return mixed, ingrad, gg[None], gu[None], gd[None]
 
 

time: 213 us -> 175 us (0.82)
  the two profiles are of different devices: /device:TPU:43 before, /device:TPU:1 now
where the time goes in v1:
time: 175 us
  Pallas kernels  174 us (99%)
    pallas_call x1, Pallas kernels, local(): pl.pallas_call(kernel, out_shape=(jax.ShapeDtypeStruct((TB, D), BF), jax....  165 us
    pallas_call x1, Pallas kernels, local(): pl.pallas_call(settle, out_shape=[jax.ShapeDtypeStruct(o.shape, o.dtype)...  8.97 us

profile of v1, /device:TPU:1, one launch (start us, length us, event | category | flops | bytes accessed | tf_op | source)
XLA Modules:
  0.0 174.8 jit_solution(17526297009247375254)
XLA Ops:
  0.6 165.2 %shard_map.110 = (bf16[128,1792]{1,0:T(8,128)(2,1)}, bf16[128,1792]{1,0:T(8,128)(2,1)}, bf16[1792,1024]{1,0:T(8,128)(2,1)}, bf16[1792,1024]{1,0:T(8,128)(2,1)}, bf16[1024,1792]{1,0:T(8,128)(2,1)}) custom-call(s32[4,128]{1,0:T(4,128)} %bitcast.11, f32[4,128]{1,0:T(4,128)} %bitcast.12, bf16[128,1792]{1,0:T(8,128)(2,1)} %tok.1, bf16[128,1792]{1,0:T(8,128)(2,1)} %cot.1, ...), custom_call_target="tpu_custom_call" | custom-call | tf_op jit(solution)/shard_map/pallas_call | solution.py:439
  165.8 9.0 %shard_map.111 = (bf16[128,1792]{1,0:T(8,128)(2,1)}, bf16[128,1792]{1,0:T(8,128)(2,1)}, bf16[1792,1024]{1,0:T(8,128)(2,1)}, bf16[1792,1024]{1,0:T(8,128)(2,1)}, bf16[1024,1792]{1,0:T(8,128)(2,1)}) custom-call(bf16[128,1792]{1,0:T(8,128)(2,1)} %get-tuple-element.15.i0, bf16[128,1792]{1,0:T(8,128)(2,1)} %get-tuple-element.16.i1, ...), custom_call_target="tpu_custom_call" | custom-call | tf_op jit(solution)/shard_map/pallas_call | solution.py:474

commit v2 on v1

--- a/solution.py
+++ b/solution.py
@@ -20,16 +20,14 @@
 HD = D // 2
 H = 1024
 ROWS = 768
-NCH = 4
-CH = ROWS // NCH
-W3 = 3 * H
-HW = W3 // 2
+Q = H // 4
 SLOTS = (
-    (0, 0), (1, 1), (1, 3), (3, 1),
-    (1, 2), (2, 1), (2, 3), (3, 2),
-    (3, 3), (2, 2), (0, 2), (2, 0),
-    (0, 1), (1, 0), (0, 3), (3, 0),
+    (1, 1), (1, 3), (3, 1), (1, 2), (2, 1), (0, 2), (2, 0),
+    (2, 2), (3, 3), (2, 3), (3, 2), (0, 1), (1, 0), (0, 3), (3, 0), (0, 0),
 )
+SIZES = (3, 4, 4, 4, 1)
+FIRST = tuple(sum(SIZES[:n]) for n in range(len(SIZES)))
+NCH = len(SIZES)
 NN = (((1,), (0,)), ((), ()))
 NT = (((1,), (1,)), ((), ()))
 TN = (((0,), (0,)), ((), ()))
@@ -42,8 +40,8 @@
 def kernel(
     routes, gates, tok, cot, wg, wu, wd,
     mixed, ingrad, ogg, ogu, ogd,
-    p1, tokp, xd_send, xd_rows, part, r1, r2, act, or_send, or_recv, pt, res, vg, vu, vd,
-    pair_s, pair_r, loc, wsem, ag_s, ag_r, ds_s, ds_r, x_s, x_r, cb_s, cb_r, fin_s, fin_r, fin_l, gsem,
+    p1, tokp, xd_send, xd_rows, part, r1, r2, act, or_send, or_recv, pt, res, cmb, vg, vu, vd,
+    pair_s, pair_r, loc, wsem, ag_s, ag_r, ds_s, ds_r, x_s, x_r, cb_s, cb_r, gv_s, gv_r, fin_s, fin_r, fin_l, gsem,
 ):
     q = lax.axis_index("dp")
     e = lax.axis_index("expert")
@@ -63,14 +61,6 @@
 
     def slot(a, b):
         return jnp.where(flip, SLOTS.index((b, a)), SLOTS.index((a, b)))
-
-    def to_chip(j):
-        dz, dy = SLOTS[j]
-        return ((cz + dz) % 4) * 4 + (cy + dy) % 4
-
-    def from_chip(j):
-        dz, dy = SLOTS[j]
-        return ((cz + 4 - dz) % 4) * 4 + (cy + 4 - dy) % 4
 
     def half(c):
         return pl.ds(pl.multiple_of(c * HD, 128), HD)
@@ -151,9 +141,15 @@
             remote(tokp.at[0], tokp.at[a], ag_s.at[a, 1], ag_r.at[a, 1], q, d),
         ]
 
-    for a in (1, 3, 2):
+    def step_s(a):
         for cp in spread(a):
             cp.start()
+
+    for a in (1, 3, 2):
+        step_s(a)
+
+    def group(a, b):
+        return pl.ds((4 * a + b) * 2 * PAIR, 2 * PAIR)
 
     def fill(a, b):
         d = chip_at(pa, pb + b)
@@ -168,8 +164,11 @@
             hit = rid == of(k)
             one = jnp.where(hit, 1.0, one)
             gat = jnp.where(hit, of(TOP + k), gat)
-        xs = mm(one.astype(BF), tokp[a, 0], NN).astype(BF)
-        dsv = mm(gat.astype(BF), tokp[a, 1], NN).astype(BF)
+        one, gat = one.astype(BF), gat.astype(BF)
+        pt[0, group(a, b)] = gat
+        pt[1, group(a, b)] = one
+        xs = mm(one, tokp[a, 0], NN).astype(BF)
+        dsv = mm(gat, tokp[a, 1], NN).astype(BF)
         xd_send[4 * a + b, :, 0] = xs.reshape(2, PAIR, HD)
         xd_send[4 * a + b, :, 1] = dsv.reshape(2, PAIR, HD)
 
@@ -190,8 +189,8 @@
 
     have = {0}
 
-    def send_chunk(c):
-        for a, b in sorted(SLOTS[4 * c : 4 * c + 4], key=lambda ab: (0, 1, 3, 2)[ab[0]]):
+    def step_f(c):
+        for a, b in sorted(SLOTS[FIRST[c] : FIRST[c] + SIZES[c]], key=lambda ab: (0, 1, 3, 2)[ab[0]]):
             if a not in have:
                 have.add(a)
                 for cp in spread(a):
@@ -200,36 +199,18 @@
             disp(a, b, 0).start()
             disp(a, b, 1).start()
 
-    for c in range(NCH):
-        send_chunk(c)
-
-    def build(n, carry):
-        r = pl.ds(pl.multiple_of(n * 128, 128), 128)
-        rid = (lax.broadcasted_iota(jnp.int32, (128, TB), 0) + n * 128).astype(F32)
-        for b in range(2):
-            one = jnp.zeros((128, TB), F32)
-            gat = jnp.zeros((128, TB), F32)
-            for k in range(TOP):
-                hit = rid == p1[0, b, k : k + 1, :]
-                one = jnp.where(hit, 1.0, one)
-                gat = jnp.where(hit, p1[0, b, TOP + k : TOP + k + 1, :], gat)
-            pt[0, r, b * TB : (b + 1) * TB] = gat.astype(BF)
-            pt[1, r, b * TB : (b + 1) * TB] = one.astype(BF)
-        return carry
-
-    lax.fori_loop(0, E * PAIR // 128, build, 0)
-
-    for cp in weights:
-        cp.wait()
+    def step_w(a):
+        for cp in weights:
+            cp.wait()
 
     def cols256(n):
         return pl.ds(pl.multiple_of(n * 256, 256), 256)
 
     def chunk(a):
-        return pl.ds(a * CH, CH)
+        return pl.ds(FIRST[a] * PAIR, SIZES[a] * PAIR)
 
     def step_a(a):
-        for sa, sb in SLOTS[4 * a : 4 * a + 4]:
+        for sa, sb in SLOTS[FIRST[a] : FIRST[a] + SIZES[a]]:
             mine_in = disp(sa, sb, 0)
             if sb == 0:
                 mine_in.wait()
@@ -237,47 +218,50 @@
                 mine_in.wait_recv()
             from_other(sa, sb).wait_recv()
 
-        def body(n, carry):
-            cs = cols256(n)
+        def body(i, carry):
+            cs = cols256((q + 2 + i) % 4)
             x = xd_rows[0, chunk(a), :]
-            part[a, :, :, cs] = mm(x, vg[:, cs], NN).astype(BF).reshape(4, PAIR, 256)
-            part[a, :, :, pl.ds(pl.multiple_of(n * 256 + H, 256), 256)] = (
-                mm(x, vu[:, cs], NN).astype(BF).reshape(4, PAIR, 256)
-            )
-            part[a, :, :, pl.ds(pl.multiple_of(n * 256 + 2 * H, 256), 256)] = (
-                mm(xd_rows[1, chunk(a), :], vd[cs, :], NT).astype(BF).reshape(4, PAIR, 256)
-            )
+            part[0, chunk(a), cs] = mm(x, vg[:, cs], NN).astype(BF)
+            part[1, chunk(a), cs] = mm(x, vu[:, cs], NN).astype(BF)
+            part[2, chunk(a), cs] = mm(xd_rows[1, chunk(a), :], vd[cs, :], NT).astype(BF)
             return carry
 
-        lax.fori_loop(0, H // 256, body, 0)
+        body(0, 0)
         for cp in rs1(a):
             cp.start()
+        lax.fori_loop(1, 4, body, 0)
+
+    def cols(n):
+        return pl.ds(pl.multiple_of(n * Q, Q), Q)
+
+    def lower(n):
+        return pl.ds(pl.multiple_of(n * Q, 128), Q // 2)
+
+    def upper(n):
+        return pl.ds(pl.multiple_of(n * Q + Q // 2, 128), Q // 2)
 
     def rs1(a):
         return [
-            remote(part.at[a, opp, :, pl.ds(0, HW)], r1.at[a, 0], x_s.at[a, 0], x_r.at[a, 0], right, e),
-            remote(part.at[a, opp, :, pl.ds(HW, HW)], r1.at[a, 1], x_s.at[a, 1], x_r.at[a, 1], left, e),
+            remote(part.at[:, chunk(a), lower(opp)], r1.at[0, :, chunk(a), :], x_s.at[a, 0], x_r.at[a, 0], right, e),
+            remote(part.at[:, chunk(a), upper(opp)], r1.at[1, :, chunk(a), :], x_s.at[a, 1], x_r.at[a, 1], left, e),
         ]
 
     def rs2(a):
         return [
-            remote(part.at[a, right], r2.at[a, 0], x_s.at[a, 2], x_r.at[a, 2], right, e),
-            remote(part.at[a, left], r2.at[a, 1], x_s.at[a, 3], x_r.at[a, 3], left, e),
+            remote(part.at[:, chunk(a), cols(right)], r2.at[0, :, chunk(a), :], x_s.at[a, 2], x_r.at[a, 2], right, e),
+            remote(part.at[:, chunk(a), cols(left)], r2.at[1, :, chunk(a), :], x_s.at[a, 3], x_r.at[a, 3], left, e),
         ]
 
-    def arow(a, n):
-        return pl.ds(pl.multiple_of(a * CH + n * PAIR, 16), PAIR)
-
     def ag1(a, n):
-        blkr = act.at[arow(a, n), :]
+        own = act.at[:, chunk(a), cols(n)]
         return [
-            remote(blkr, blkr, x_s.at[a, 4], x_r.at[a, 4], right, e),
-            remote(blkr, blkr, x_s.at[a, 5], x_r.at[a, 5], left, e),
+            remote(own, own, x_s.at[a, 4], x_r.at[a, 4], right, e),
+            remote(own, own, x_s.at[a, 5], x_r.at[a, 5], left, e),
         ]
 
     def ag2(a, n0, n1):
-        b0 = act.at[arow(a, n0), pl.ds(0, HW)]
-        b1 = act.at[arow(a, n1), pl.ds(HW, HW)]
+        b0 = act.at[:, chunk(a), lower(n0)]
+        b1 = act.at[:, chunk(a), upper(n1)]
         return [
             remote(b0, b0, x_s.at[a, 6], x_r.at[a, 6], right, e),
             remote(b1, b1, x_s.at[a, 7], x_r.at[a, 7], left, e),
@@ -287,24 +271,23 @@
         for cp in rs1(a):
             cp.wait_recv()
         s2 = rs2(a)
-        part[a, right, :, 0:HW] = (part[a, right, :, 0:HW].astype(F32) + r1[a, 0].astype(F32)).astype(BF)
+        part[:, chunk(a), lower(right)] = (part[:, chunk(a), lower(right)].astype(F32) + r1[0, :, chunk(a), :].astype(F32)).astype(BF)
         s2[0].start()
-        part[a, left, :, HW:W3] = (part[a, left, :, HW:W3].astype(F32) + r1[a, 1].astype(F32)).astype(BF)
+        part[:, chunk(a), upper(left)] = (part[:, chunk(a), upper(left)].astype(F32) + r1[1, :, chunk(a), :].astype(F32)).astype(BF)
         s2[1].start()
 
     def step_c(a):
         for cp in rs2(a):
             cp.wait_recv()
 
-        def total(lo):
-            s = slice(lo, lo + H)
-            return part[a, q, :, s].astype(F32) + r2[a, 0, :, s].astype(F32) + r2[a, 1, :, s].astype(F32)
-
-        g, u, hg = total(0), total(H), total(2 * H)
+        def total(k):
+            return part[k, chunk(a), cols(q)].astype(F32) + r2[0, k, chunk(a), :].astype(F32) + r2[1, k, chunk(a), :].astype(F32)
+
+        g, u, hg = total(0), total(1), total(2)
         sig = jax.nn.sigmoid(g)
-        act[arow(a, q), 0:H] = (g * sig * u).astype(BF)
-        act[arow(a, q), H : 2 * H] = (hg * u * sig * (1.0 + g * (1.0 - sig))).astype(BF)
-        act[arow(a, q), 2 * H : W3] = (hg * g * sig).astype(BF)
+        act[0, chunk(a), cols(q)] = (g * sig * u).astype(BF)
+        act[1, chunk(a), cols(q)] = (hg * u * sig * (1.0 + g * (1.0 - sig))).astype(BF)
+        act[2, chunk(a), cols(q)] = (hg * g * sig).astype(BF)
         for cp in ag1(a, q):
             cp.start()
 
@@ -314,14 +297,42 @@
         for cp in ag2(a, left, right):
             cp.start()
 
-    def comb(j, k, dst_chip, src_e):
-        c_dst = core if k == 0 else other
-        return remote(
-            or_send.at[:, rows48(j), half(c_dst)], or_recv.at[:, rows48(src_e), :],
-            cb_s.at[j, k], cb_r.at[j, k], q, dst_chip * 2 + c_dst,
-        )
-
-    own_back = pltpu.make_async_copy(or_send.at[:, rows48(0), half(core)], or_recv.at[:, rows48(e), :], loc.at[5])
+    def comb(a, b, k):
+        rows = rows48(slot(a, b))
+        n = 4 * a + b if k == 0 else 4 * b + a
+        dst = or_recv.at[:, pl.ds(pl.multiple_of(n * 2 * PAIR + core * PAIR, 16), PAIR), :]
+        if k == 0:
+            src = or_send.at[:, rows, half(core)]
+            if b == 0:
+                return pltpu.make_async_copy(src, dst, cb_r.at[n, 0])
+            return remote(src, dst, cb_s.at[n, 0], cb_r.at[n, 0], q, chip_at(pa, pb + 4 - b) * 2 + core)
+        src = or_send.at[:, rows, half(other)]
+        return remote(src, dst, cb_s.at[n, 1], cb_r.at[n, 1], q, chip_at(pa + 4 - a, pb) * 2 + other)
+
+    def comb_other(a, b):
+        n = 4 * a + b
+        dst = or_recv.at[:, pl.ds(pl.multiple_of(n * 2 * PAIR + other * PAIR, 16), PAIR), :]
+        return remote(or_send.at[:, rows48(0), half(core)], dst, cb_s.at[n, 1], cb_r.at[n, 1], q, partner)
+
+    def give(a):
+        return remote(tokp.at[a], cmb.at[a - 1], gv_s.at[a], gv_r.at[a], q, chip_at(pa + 4 - a, pb) * 2 + core)
+
+    def added(a, k):
+        r = pl.ds(a * 8 * PAIR, 8 * PAIR)
+        return mm(pt[k, r, :], or_recv[k, r, :], TN)
+
+    def step_g(a):
+        for b in range(4):
+            cp = comb(a, b, 0)
+            if b == 0:
+                cp.wait()
+            else:
+                cp.wait_recv()
+            comb_other(a, b).wait_recv()
+        if a != 0:
+            for k in range(2):
+                tokp[a, k] = added(a, k).astype(BF)
+            give(a).start()
 
     def step_e(a):
         for cp in ag2(a, opp, opp):
@@ -329,33 +340,27 @@
 
         def body(n, carry):
             cs = cols256(n)
-            or_send[0, chunk(a), cs] = mm(act[chunk(a), 0:H], vd[:, cs], NN).astype(BF)
+            or_send[0, chunk(a), cs] = mm(act[0, chunk(a), :], vd[:, cs], NN).astype(BF)
             or_send[1, chunk(a), cs] = (
-                mm(act[chunk(a), H : 2 * H], vg[cs, :], NT) + mm(act[chunk(a), 2 * H : W3], vu[cs, :], NT)
+                mm(act[1, chunk(a), :], vg[cs, :], NT) + mm(act[2, chunk(a), :], vu[cs, :], NT)
             ).astype(BF)
             return carry
 
         lax.fori_loop(0, D // 256, body, 0)
-        for j in range(4 * a, 4 * a + 4):
-            d = from_chip(j)
-            if j == 0:
-                own_back.start()
-            else:
-                comb(j, 0, d, e).start()
-            comb(j, 1, d, e).start()
+        for sa, sb in SLOTS[FIRST[a] : FIRST[a] + SIZES[a]]:
+            comb(sa, sb, 0).start()
+            comb(sa, sb, 1).start()
 
     for step, a in (
-        (step_a, 0), (step_b, 0), (step_c, 0), (step_a, 1), (step_d, 0), (step_b, 1), (step_e, 0), (step_c, 1),
-        (step_a, 2), (step_d, 1), (step_b, 2), (step_e, 1), (step_c, 2), (step_a, 3), (step_d, 2), (step_b, 3),
-        (step_e, 2), (step_c, 3), (step_d, 3), (step_e, 3),
+        (step_f, 0), (step_f, 1), (step_f, 2), (step_w, 0), (step_a, 0), (step_f, 3), (step_b, 0), (step_f, 4), (step_a, 1), (step_c, 0), (step_b, 1), (step_d, 0), (step_a, 2), (step_c, 1), (step_e, 0), (step_b, 2), (step_d, 1), (step_a, 3), (step_c, 2), (step_e, 1), (step_b, 3), (step_d, 2), (step_a, 4), (step_c, 3), (step_e, 2), (step_b, 4), (step_d, 3), (step_c, 4), (step_e, 3), (step_g, 2), (step_d, 4), (step_g, 1), (step_g, 3), (step_e, 4),
     ):
         step(a)
 
     def grad_x(n, carry):
         cs = cols256(n)
         x = xd_rows[0, :, cs]
-        vg[cs, :] = mm(x, act[:, H : 2 * H], TN).astype(BF)
-        vu[cs, :] = mm(x, act[:, 2 * H : W3], TN).astype(BF)
+        vg[cs, :] = mm(x, act[1], TN).astype(BF)
+        vu[cs, :] = mm(x, act[2], TN).astype(BF)
         return carry
 
     lax.fori_loop(0, D // 256, grad_x, 0)
@@ -369,20 +374,18 @@
 
     def grad_d(n, carry):
         cs = cols256(n)
-        vd[cs, :] = mm(act[:, cs], xd_rows[1], TN).astype(BF)
+        vd[cs, :] = mm(act[0, :, cs], xd_rows[1], TN).astype(BF)
         return carry
 
     lax.fori_loop(0, H // 256, grad_d, 0)
     out_w[2].start()
 
-    own_back.wait()
-    for j in range(16):
-        src = to_chip(j)
-        if j > 0:
-            comb(j, 0, chip, src * 2 + core).wait_recv()
-        comb(j, 1, chip, src * 2 + other).wait_recv()
-    res[0] = mm(pt[0], or_recv[0], TN).astype(BF)
-    res[1] = mm(pt[1], or_recv[1], TN).astype(BF)
+    step_g(0)
+    for a in (2, 1, 3):
+        give(a).wait_recv()
+    for k in range(2):
+        far = cmb[0, k].astype(F32) + cmb[1, k].astype(F32) + cmb[2, k].astype(F32)
+        res[k] = (added(0, k) + far).astype(BF)
     fin = []
     for k, out in enumerate((mixed, ingrad)):
         away = remote(res.at[k, blk(other), :], out.at[:, half(core)], fin_s.at[k], fin_r.at[k], q, partner)
@@ -400,10 +403,12 @@
         if b != 0:
             disp(a, b, 0).wait_send()
         disp(a, b, 1).wait_send()
-    for j in range(16):
-        if j > 0:
-            comb(j, 0, chip, e).wait_send()
-        comb(j, 1, chip, e).wait_send()
+    for a, b in SLOTS:
+        if b != 0:
+            comb(a, b, 0).wait_send()
+        comb(a, b, 1).wait_send()
+    for a in (1, 2, 3):
+        give(a).wait_send()
     for a in range(NCH):
         for cp in rs1(a) + rs2(a) + ag1(a, q) + ag2(a, left, right):
             cp.wait_send()
@@ -452,20 +457,21 @@
             pltpu.VMEM((4, 2, 2 * TB, HD), BF),
             pltpu.VMEM((16, 2, 2, PAIR, HD), BF),
             pltpu.VMEM((2, ROWS, D), BF),
-            pltpu.VMEM((NCH, 4, PAIR, W3), BF),
-            pltpu.VMEM((NCH, 2, PAIR, HW), BF),
-            pltpu.VMEM((NCH, 2, PAIR, W3), BF),
-            pltpu.VMEM((ROWS, W3), BF),
+            pltpu.VMEM((3, ROWS, H), BF),
+            pltpu.VMEM((2, 3, ROWS, Q // 2), BF),
+            pltpu.VMEM((2, 3, ROWS, Q), BF),
+            pltpu.VMEM((3, ROWS, H), BF),
             pltpu.VMEM((2, ROWS, D), BF),
             pltpu.VMEM((2, E * PAIR, HD), BF),
             pltpu.VMEM((2, E * PAIR, 2 * TB), BF),
             pltpu.VMEM((2, 2 * TB, HD), BF),
+            pltpu.VMEM((3, 2, 2 * TB, HD), BF),
             pltpu.VMEM((D, H), BF),
             pltpu.VMEM((D, H), BF),
             pltpu.VMEM((H, D), BF),
             dma((4,)), dma((4,)), dma((6,)), dma((3,)), dma((4, 2)), dma((4, 2)),
             dma((16, 2)), dma((16, 2)), dma((NCH, 8)), dma((NCH, 8)),
-            dma((16, 2)), dma((16, 2)), dma((2,)), dma((2,)), dma((2,)), dma((3,)),
+            dma((16, 2)), dma((16, 2)), dma((4,)), dma((4,)), dma((2,)), dma((2,)), dma((2,)), dma((3,)),
         ],
         compiler_params=pltpu.CompilerParams(
             collective_id=0, has_side_effects=True, vmem_limit_bytes=62 * 1024 * 1024

time: 175 us -> 169 us (0.966)
  Pallas kernels: 174 us -> 168 us
    pallas_call x1, Pallas kernels: 165 us -> 159 us  [local(): pl.pallas_call(kernel, out_shape=(jax.ShapeDtypeStruct((TB, D), BF), jax....]
where the time goes in v2:
time: 169 us
  Pallas kernels  168 us (99%)
    pallas_call x1, Pallas kernels, local(): pl.pallas_call(kernel, out_shape=(jax.ShapeDtypeStruct((TB, D), BF), jax....  159 us
    pallas_call x1, Pallas kernels, local(): pl.pallas_call(settle, out_shape=[jax.ShapeDtypeStruct(o.shape, o.dtype)...  8.97 us

profile of v2, /device:TPU:1, one launch (start us, length us, event | category | flops | bytes accessed | tf_op | source)
XLA Modules:
  0.0 168.8 jit_solution(6432533126035845030)
XLA Ops:
  0.6 159.0 %shard_map.110 = (bf16[128,1792]{1,0:T(8,128)(2,1)}, bf16[128,1792]{1,0:T(8,128)(2,1)}, bf16[1792,1024]{1,0:T(8,128)(2,1)}, bf16[1792,1024]{1,0:T(8,128)(2,1)}, bf16[1024,1792]{1,0:T(8,128)(2,1)}) custom-call(s32[4,128]{1,0:T(4,128)} %bitcast.11, f32[4,128]{1,0:T(4,128)} %bitcast.12, bf16[128,1792]{1,0:T(8,128)(2,1)} %tok.1, bf16[128,1792]{1,0:T(8,128)(2,1)} %cot.1, ...), custom_call_target="tpu_custom_call" | custom-call | tf_op jit(solution)/shard_map/pallas_call | solution.py:444
  159.6 9.0 %shard_map.111 = (bf16[128,1792]{1,0:T(8,128)(2,1)}, bf16[128,1792]{1,0:T(8,128)(2,1)}, bf16[1792,1024]{1,0:T(8,128)(2,1)}, bf16[1792,1024]{1,0:T(8,128)(2,1)}, bf16[1024,1792]{1,0:T(8,128)(2,1)}) custom-call(bf16[128,1792]{1,0:T(8,128)(2,1)} %get-tuple-element.15.i0, bf16[128,1792]{1,0:T(8,128)(2,1)} %get-tuple-element.16.i1, ...), custom_call_target="tpu_custom_call" | custom-call | tf_op jit(solution)/shard_map/pallas_call | solution.py:480

commit v3 on v2

--- a/solution.py
+++ b/solution.py
@@ -135,6 +135,13 @@
         cp.wait_recv()
 
     def spread(a):
+        if a == 2:
+            up, down = chip_at(pa + 1, pb) * 2 + core, chip_at(pa + 3, pb) * 2 + core
+            return [
+                remote(p1.at[1], p1.at[2], ag_s.at[2, 0], ag_r.at[2, 0], q, up),
+                remote(tokp.at[1, 0], tokp.at[2, 0], ag_s.at[2, 1], ag_r.at[2, 1], q, up),
+                remote(tokp.at[3, 1], tokp.at[2, 1], ag_s.at[2, 2], ag_r.at[2, 2], q, down),
+            ]
         d = chip_at(pa + a, pb) * 2 + core
         return [
             remote(p1.at[0], p1.at[a], ag_s.at[a, 0], ag_r.at[a, 0], q, d),
@@ -145,7 +152,7 @@
         for cp in spread(a):
             cp.start()
 
-    for a in (1, 3, 2):
+    for a in (1, 3):
         step_s(a)
 
     def group(a, b):
@@ -314,6 +321,13 @@
         dst = or_recv.at[:, pl.ds(pl.multiple_of(n * 2 * PAIR + other * PAIR, 16), PAIR), :]
         return remote(or_send.at[:, rows48(0), half(core)], dst, cb_s.at[n, 1], cb_r.at[n, 1], q, partner)
 
+    def give_far():
+        down, up = chip_at(pa + 3, pb) * 2 + core, chip_at(pa + 1, pb) * 2 + core
+        return [
+            remote(tokp.at[2, 0], cmb.at[1, 0], gv_s.at[0], gv_r.at[0], q, down),
+            remote(tokp.at[2, 1], cmb.at[1, 1], gv_s.at[2], gv_r.at[2], q, up),
+        ]
+
     def give(a):
         return remote(tokp.at[a], cmb.at[a - 1], gv_s.at[a], gv_r.at[a], q, chip_at(pa + 4 - a, pb) * 2 + core)
 
@@ -322,6 +336,9 @@
         return mm(pt[k, r, :], or_recv[k, r, :], TN)
 
     def step_g(a):
+        if a == 2:
+            for cp in spread(2):
+                cp.wait_send()
         for b in range(4):
             cp = comb(a, b, 0)
             if b == 0:
@@ -329,10 +346,17 @@
             else:
                 cp.wait_recv()
             comb_other(a, b).wait_recv()
-        if a != 0:
-            for k in range(2):
-                tokp[a, k] = added(a, k).astype(BF)
-            give(a).start()
+        if a == 0:
+            return
+        passing = {1: 0, 3: 1}.get(a)
+        for k in range(2):
+            sums = added(a, k)
+            if k == passing:
+                give_far()[k].wait_recv()
+                sums = sums + cmb[1, k].astype(F32)
+            tokp[a, k] = sums.astype(BF)
+        for cp in give_far() if a == 2 else [give(a)]:
+            cp.start()
 
     def step_e(a):
         for cp in ag2(a, opp, opp):
@@ -352,7 +376,7 @@
             comb(sa, sb, 1).start()
 
     for step, a in (
-        (step_f, 0), (step_f, 1), (step_f, 2), (step_w, 0), (step_a, 0), (step_f, 3), (step_b, 0), (step_f, 4), (step_a, 1), (step_c, 0), (step_b, 1), (step_d, 0), (step_a, 2), (step_c, 1), (step_e, 0), (step_b, 2), (step_d, 1), (step_a, 3), (step_c, 2), (step_e, 1), (step_b, 3), (step_d, 2), (step_a, 4), (step_c, 3), (step_e, 2), (step_b, 4), (step_d, 3), (step_c, 4), (step_e, 3), (step_g, 2), (step_d, 4), (step_g, 1), (step_g, 3), (step_e, 4),
+        (step_f, 0), (step_s, 2), (step_f, 1), (step_f, 2), (step_w, 0), (step_a, 0), (step_f, 3), (step_b, 0), (step_f, 4), (step_a, 1), (step_c, 0), (step_b, 1), (step_d, 0), (step_a, 2), (step_c, 1), (step_e, 0), (step_b, 2), (step_d, 1), (step_a, 3), (step_c, 2), (step_e, 1), (step_b, 3), (step_d, 2), (step_a, 4), (step_c, 3), (step_e, 2), (step_b, 4), (step_d, 3), (step_c, 4), (step_e, 3), (step_g, 2), (step_d, 4), (step_g, 1), (step_g, 3), (step_e, 4),
     ):
         step(a)
 
@@ -381,10 +405,10 @@
     out_w[2].start()
 
     step_g(0)
-    for a in (2, 1, 3):
+    for a in (1, 3):
         give(a).wait_recv()
     for k in range(2):
-        far = cmb[0, k].astype(F32) + cmb[1, k].astype(F32) + cmb[2, k].astype(F32)
+        far = cmb[0, k].astype(F32) + cmb[2, k].astype(F32)
         res[k] = (added(0, k) + far).astype(BF)
     fin = []
     for k, out in enumerate((mixed, ingrad)):
@@ -396,7 +420,7 @@
 
     for cp in mine + [pair_rows(core)]:
         cp.wait_send()
-    for a in (1, 2, 3):
+    for a in (1, 3):
         for cp in spread(a):
             cp.wait_send()
     for a, b in SLOTS:
@@ -407,8 +431,8 @@
         if b != 0:
             comb(a, b, 0).wait_send()
         comb(a, b, 1).wait_send()
-    for a in (1, 2, 3):
-        give(a).wait_send()
+    for cp in [give(1), give(3)] + give_far():
+        cp.wait_send()
     for a in range(NCH):
         for cp in rs1(a) + rs2(a) + ag1(a, q) + ag2(a, left, right):
             cp.wait_send()
@@ -469,7 +493,7 @@
             pltpu.VMEM((D, H), BF),
             pltpu.VMEM((D, H), BF),
             pltpu.VMEM((H, D), BF),
-            dma((4,)), dma((4,)), dma((6,)), dma((3,)), dma((4, 2)), dma((4, 2)),
+            dma((4,)), dma((4,)), dma((6,)), dma((3,)), dma((4, 3)), dma((4, 3)),
             dma((16, 2)), dma((16, 2)), dma((NCH, 8)), dma((NCH, 8)),
             dma((16, 2)), dma((16, 2)), dma((4,)), dma((4,)), dma((2,)), dma((2,)), dma((2,)), dma((3,)),
         ],

time: 169 us -> 168 us (level)
  no operation moved by 1% of the time
where the time goes in v3:
time: 168 us
  Pallas kernels  167 us (99%)
    pallas_call x1, Pallas kernels, local(): pl.pallas_call(kernel, out_shape=(jax.ShapeDtypeStruct((TB, D), BF), jax....  158 us
    pallas_call x1, Pallas kernels, local(): pl.pallas_call(settle, out_shape=[jax.ShapeDtypeStruct(o.shape, o.dtype)...  8.97 us

profile of v3, /device:TPU:1, one launch (start us, length us, event | category | flops | bytes accessed | tf_op | source)
XLA Modules:
  0.0 167.5 jit_solution(11915183189678122035)
XLA Ops:
  0.6 157.7 %shard_map.110 = (bf16[128,1792]{1,0:T(8,128)(2,1)}, bf16[128,1792]{1,0:T(8,128)(2,1)}, bf16[1792,1024]{1,0:T(8,128)(2,1)}, bf16[1792,1024]{1,0:T(8,128)(2,1)}, bf16[1024,1792]{1,0:T(8,128)(2,1)}) custom-call(s32[4,128]{1,0:T(4,128)} %bitcast.11, f32[4,128]{1,0:T(4,128)} %bitcast.12, bf16[128,1792]{1,0:T(8,128)(2,1)} %tok.1, bf16[128,1792]{1,0:T(8,128)(2,1)} %cot.1, ...), custom_call_target="tpu_custom_call" | custom-call | tf_op jit(solution)/shard_map/pallas_call | solution.py:468
  158.4 9.0 %shard_map.111 = (bf16[128,1792]{1,0:T(8,128)(2,1)}, bf16[128,1792]{1,0:T(8,128)(2,1)}, bf16[1792,1024]{1,0:T(8,128)(2,1)}, bf16[1792,1024]{1,0:T(8,128)(2,1)}, bf16[1024,1792]{1,0:T(8,128)(2,1)}) custom-call(bf16[128,1792]{1,0:T(8,128)(2,1)} %get-tuple-element.15.i0, bf16[128,1792]{1,0:T(8,128)(2,1)} %get-tuple-element.16.i1, ...), custom_call_target="tpu_custom_call" | custom-call | tf_op jit(solution)/shard_map/pallas_call | solution.py:504

commit v4 on v3

--- a/solution.py
+++ b/solution.py
@@ -407,11 +407,10 @@
     step_g(0)
     for a in (1, 3):
         give(a).wait_recv()
-    for k in range(2):
+    fin = []
+    for k, out in enumerate((mixed, ingrad)):
         far = cmb[0, k].astype(F32) + cmb[2, k].astype(F32)
         res[k] = (added(0, k) + far).astype(BF)
-    fin = []
-    for k, out in enumerate((mixed, ingrad)):
         away = remote(res.at[k, blk(other), :], out.at[:, half(core)], fin_s.at[k], fin_r.at[k], q, partner)
         here = pltpu.make_async_copy(res.at[k, blk(core), :], out.at[:, half(core)], fin_l.at[k])
         away.start()

time: 168 us -> 168 us (level)
  no operation moved by 1% of the time
where the time goes in v4:
time: 168 us; the launch traced here: 167 us
  Pallas kernels  167 us (99%)
    pallas_call x1, Pallas kernels, local(): pl.pallas_call(kernel, out_shape=(jax.ShapeDtypeStruct((TB, D), BF), jax....  158 us
    pallas_call x1, Pallas kernels, local(): pl.pallas_call(settle, out_shape=[jax.ShapeDtypeStruct(o.shape, o.dtype)...  8.97 us

profile of v4, /device:TPU:1, one launch (start us, length us, event | category | flops | bytes accessed | tf_op | source)
XLA Modules:
  0.0 167.4 jit_solution(3262069016521827766)
XLA Ops:
  0.6 157.6 %shard_map.110 = (bf16[128,1792]{1,0:T(8,128)(2,1)}, bf16[128,1792]{1,0:T(8,128)(2,1)}, bf16[1792,1024]{1,0:T(8,128)(2,1)}, bf16[1792,1024]{1,0:T(8,128)(2,1)}, bf16[1024,1792]{1,0:T(8,128)(2,1)}) custom-call(s32[4,128]{1,0:T(4,128)} %bitcast.11, f32[4,128]{1,0:T(4,128)} %bitcast.12, bf16[128,1792]{1,0:T(8,128)(2,1)} %tok.1, bf16[128,1792]{1,0:T(8,128)(2,1)} %cot.1, ...), custom_call_target="tpu_custom_call" | custom-call | tf_op jit(solution)/shard_map/pallas_call | solution.py:467
  158.3 9.0 %shard_map.111 = (bf16[128,1792]{1,0:T(8,128)(2,1)}, bf16[128,1792]{1,0:T(8,128)(2,1)}, bf16[1792,1024]{1,0:T(8,128)(2,1)}, bf16[1792,1024]{1,0:T(8,128)(2,1)}, bf16[1024,1792]{1,0:T(8,128)(2,1)}) custom-call(bf16[128,1792]{1,0:T(8,128)(2,1)} %get-tuple-element.15.i0, bf16[128,1792]{1,0:T(8,128)(2,1)} %get-tuple-element.16.i1, ...), custom_call_target="tpu_custom_call" | custom-call | tf_op jit(solution)/shard_map/pallas_call | solution.py:503
